TPU v7x, 256 devices: a whole 4x4x8 slice. The times are simulated.
256 devices in a mesh: depth: 2 (over z_lo), row: 8 (over x, core), col: 16 (over z_hi, y).
Axes of the slice: x: 4, y: 4, z: 8 (z_hi: 4, z_lo: 2; z = z_hi * 2 + z_lo), core: 2. Of those that a mesh axis runs over, the one named last changes fastest.
Arguments:
- normed: bfloat16 [4096, 6144], P(('depth', 'col'), 'row'), may hold values from -6 to 6
- positions: int32 [4096], P(('depth', 'col')), may hold values from 0 to 1567, as said below
- cotangent: bfloat16 [4096, 6144], P(('depth', 'col'), 'row'), may hold values from -4 to 4
- w_in: bfloat16 [6144, 12288], P('row', 'col'), may hold values from -0.078125 to 0.078125
- b_in: float32 [12288], P('col'), may hold values from -4 to 4
- w_out: bfloat16 [12288, 6144], P('col', 'row'), may hold values from -0.0546875 to 0.0546875
Outputs:
- d_normed: bfloat16 [4096, 6144], P(('depth', 'col'), 'row')
- d_w_in: float32 [6144, 12288], P('row', 'col')
- d_b_in: float32 [12288], P('col')
- d_w_out: float32 [12288, 6144], P('col', 'row')
Inputs may be any that keep to these rules, and one draw needn't show every extreme that they name: positions holds 16 clips of 256 consecutive tokens; in each clip the same 256 // 8 of the 196 spatial places (ascending, always including places 0 and 195) are kept in each of the 8 frames, position = frame * 196 + place, frames ascending.
All inputs are finite; a program needn't handle non-finite values.
Results may differ from a plain program's by a relative error of at most 0.03.
Values may be sent and summed in bfloat16 or wider, within the bound.
No kernel may reach another device: no remote copies, remote signals or barrier semaphores. Data moves between devices by JAX's collectives and lax.ppermute only.
A program may use at most 128 MiB of HBM per device.

v0:
```python
import jax
import jax.numpy as jnp
from jax import lax
from jax.sharding import PartitionSpec as P

D = 6144
AXES = ("depth", "row", "col")

coeff = 0.7978845608028654


def sincos(positions, first, width):
    places = positions.astype(jnp.float32)[:, None]
    column = first + jnp.arange(width, dtype=jnp.int32)
    expo = (2 * (column // 2)).astype(jnp.float32) / jnp.float32(D)
    freq = jnp.power(jnp.float32(10000.0), -expo)
    angle = places * freq[None, :]
    return jnp.where((column % 2 == 0)[None, :], jnp.sin(angle), jnp.cos(angle))


def gelu_pair(value):
    inner = coeff * (value + 0.044715 * value * value * value)
    slope = jnp.tanh(inner)
    out = 0.5 * value * (1.0 + slope)
    grad = 0.5 * (1.0 + slope) + 0.5 * value * (1.0 - slope * slope) * coeff * (
        1.0 + 3.0 * 0.044715 * value * value
    )
    return (out, grad)


def moves(shift):
    def index(d, x, c, z, y):
        return ((d % 2) * 8 + (x % 4) * 2 + c % 2) * 16 + (z % 4) * 4 + y % 4

    return [
        (index(d, x, c, z, y), index(*shift(d, x, c, z, y)))
        for d in range(2)
        for x in range(4)
        for c in range(2)
        for z in range(4)
        for y in range(4)
    ]


CORE = moves(lambda d, x, c, z, y: (d, x, c + 1, z, y))
DEPTH = moves(lambda d, x, c, z, y: (d + 1, x, c, z, y))
Y_BY = [moves(lambda d, x, c, z, y, k=k: (d, x, c, z, y + k)) for k in range(4)]
Z_BY = [moves(lambda d, x, c, z, y, j=j: (d, x, c, z + j, y)) for j in range(4)]
X_SETS = [[c + 2 * x for x in range(4)] for c in range(2)]

Y_SETS = [[z * 4 + y for y in range(4)] for z in range(4)]
IN_GROUPS = ((0, 1, 3), (2,))


def send(value, pairs):
    return lax.ppermute(value, AXES, pairs)


def dot(a, b, contract, kind=jnp.float32):
    return lax.dot_general(
        a, b, ((contract[:1], contract[1:]), ((), ())), preferred_element_type=jnp.float32
    ).astype(kind)


def on_device(normed, positions, cotangent, w_in, b_in, w_out):
    bf, f32 = jnp.bfloat16, jnp.float32
    width = w_in.shape[0]
    hidden = w_in.shape[1]
    row = lax.axis_index("row")
    core = row % 2
    half = normed.shape[0] // 2

    def after(value, *others):
        return lax.optimization_barrier((value, *others))[0]

    def gather_z(value):
        return jnp.concatenate([value] + [send(value, Z_BY[4 - j]) for j in range(1, 4)], axis=0)

    def swap_x(value):
        return lax.all_to_all(value, "row", 0, 0, tiled=True, axis_index_groups=X_SETS)

    def scatter_x(part):
        return jnp.sum(swap_x(part).astype(f32), axis=0)

    def gather_x(own):
        return swap_x(jnp.broadcast_to(own[None], (4,) + own.shape))

    inputs = (normed.astype(f32) + sincos(positions, row * width, width)).astype(bf)
    both = jnp.stack([inputs, cotangent])
    mine = lax.dynamic_slice_in_dim(both, core * half, half, 1)
    other = send(lax.dynamic_slice_in_dim(both, (1 - core) * half, half, 1), CORE)
    x_half = jnp.concatenate([mine[0], other[0]], axis=1)
    c_half = jnp.concatenate([mine[1], other[1]], axis=1)
    w_in_got = send(w_in, CORE)
    w_out_got = send(w_out, CORE)
    w_in_all = jnp.concatenate([w_in, w_in_got], axis=0)
    w_out_all = jnp.concatenate([w_out, w_out_got], axis=1)

    x_own = gather_z(x_half)
    c_four = lax.all_to_all(
        jnp.broadcast_to(c_half[None], (4,) + c_half.shape), "col", 0, 0, tiled=True, axis_index_groups=Y_SETS
    )
    y = lax.axis_index("col") % 4
    c_own = lax.dynamic_slice_in_dim(jnp.concatenate([c_four, c_four]), y, 4, 0)

    x_own = after(x_own, c_four)
    x_up, x_down = send(x_own, Y_BY[3]), send(x_own, Y_BY[1])
    c_own = after(c_own, x_own, w_in_got, w_out_got)
    c_up, c_down = send(c_own, Z_BY[3]), send(c_own, Z_BY[1])
    xs = [x_own, x_up, None, x_down]
    parts = [dot(x_own, w_in_all, (1, 0), bf), None, None, None]
    x_up, x_down = after((x_up, x_down), parts[0])
    rows = 2 * half
    xs[1], xs[3] = x_up, x_down
    xs[2] = jnp.concatenate([send(x_up[:rows], Y_BY[3]), send(x_down[rows:], Y_BY[1])])
    acts, slopes = [None] * 4, [None] * 4
    pre = None
    for g in IN_GROUPS:
        for k in g:
            if parts[k] is None:
                parts[k] = dot(xs[k], w_in_all, (1, 0), bf)
        part = jnp.stack([parts[k].reshape(4, half, hidden) for k in g], axis=1)
        pre = scatter_x(part if pre is None else after(part, pre)) + b_in[None, None, :]
        act, slope = gelu_pair(pre)
        for i, k in enumerate(g):
            acts[k], slopes[k] = act[i], slope[i]
    act_all = gather_x(jnp.stack(acts).astype(bf))

    c_up, c_down = after((c_up, c_down), parts[2])
    c_far = jnp.concatenate([send(c_up[:2], Z_BY[3]), send(c_down[2:], Z_BY[1])])
    cs = [c.reshape(-1, 2 * width) for c in (c_own, c_up, c_far, c_down)]
    d_parts = jnp.stack([dot(c, w_out_all, (1, 1), bf).reshape(4, half, hidden) for c in cs])
    d_act = scatter_x(after(d_parts, act_all))
    d_pre_all = gather_x((d_act * jnp.stack(slopes)).astype(bf))

    act_all = act_all.reshape(-1, hidden)
    c_mine = jnp.concatenate([c[:, :width] for c in cs])
    c_other = jnp.concatenate([c[:, width:] for c in cs])
    out_got = send(dot(act_all, c_other, (0, 0), bf), CORE)
    out_mine = (dot(act_all, c_mine, (0, 0)) + out_got.astype(f32)).astype(bf)
    out_deep = send(out_mine, DEPTH)
    d_w_out = out_mine.astype(f32) + out_deep.astype(f32)

    d_pre_all = after(d_pre_all, out_mine).swapaxes(0, 1)
    d_pres = [d_pre_all[k].reshape(4 * half, hidden) for k in range(4)]
    shares = [dot(d_pres[k], w_in_all, (1, 1), bf) for k in (1, 3, 2)]
    d_pre_all = after(d_pre_all, out_deep, *shares)
    d_pre_rows = d_pre_all.reshape(-1, hidden)
    x_mine = jnp.concatenate([x[:, :width] for x in xs])
    x_other = jnp.concatenate([x[:, width:] for x in xs])
    x_other = jnp.concatenate([x_other, jnp.ones((x_other.shape[0], 16), bf)], axis=1)
    in_other = dot(x_other, d_pre_rows, (0, 0), bf)
    in_got = send(in_other, CORE)
    in_mine = (dot(x_mine, d_pre_rows, (0, 0)) + in_got[:width].astype(f32)).astype(bf)
    bias = (in_other[width:].astype(f32) + in_got[width:].astype(f32)).astype(bf)
    in_mine = jnp.concatenate([in_mine, bias])
    d_in = in_mine.astype(f32) + send(in_mine, DEPTH).astype(f32)
    d_w_in, d_b_in = d_in[:width], d_in[width]

    total = dot(d_pres[0], w_in_all, (1, 1))
    for k, share in zip((1, 3, 2), shares):
        total = total + send(share, Y_BY[k]).astype(f32)
    total = total.reshape(4, half, 2 * width)
    d_half = total[0]
    for j in range(1, 4):
        d_half = d_half + send(total[j].astype(bf), Z_BY[j]).astype(f32)
    d_half = d_half.astype(bf)
    mine, got = d_half[:, :width], send(d_half[:, width:], CORE)
    first = jnp.where(core == 0, mine, got)
    second = jnp.where(core == 0, got, mine)
    d_normed = jnp.concatenate([first, second], axis=0)
    return (d_normed, d_w_in, d_b_in, d_w_out)


def solution(mesh):
    placed = (
        P(("depth", "col"), "row"),
        P(("depth", "col")),
        P(("depth", "col"), "row"),
        P("row", "col"),
        P("col"),
        P("col", "row"),
    )
    return jax.shard_map(
        on_device,
        mesh=mesh,
        in_specs=placed,
        out_specs=(P(("depth", "col"), "row"), P("row", "col"), P("col"), P("col", "row")),
        check_vma=False,
    )
```

profile of v0, /device:TPU:1, one launch (start us, length us, event | category | flops | bytes accessed | tf_op | source)
XLA Modules:
  0.0 247.3 jit_solution(8213112004109302283)
XLA Ops:
  4.8 3.3 %collective-permute-start = (bf16[2,64,768]{2,1,0:T(8,128)(2,1)S(1)}, bf16[2,64,768]{2,1,0:T(8,128)(2,1)S(1)}, u32[]{:S(2)}, u32[]{:S(2)}) collective-permute-start(bf16[2,64,768]{2,1,0:T(8,128)(2,1)S(1)} %get-tuple-element.50), channel_id=1, source_target_pairs={{0,16},{1,17},{2,18},{3,19},{4,20},{5,21},{6,22},{7,23},{8,24},{9,... | collective-permute-start | bytes 589832 | tf_op jit(solution)/shard_map/ppermute | solution.py:56
  10.2 4.2 %all-to-all-start = ((bf16[4,64,1536]{2,1,0:T(8,128)(2,1)}), bf16[4,64,1536]{2,1,0:T(8,128)(2,1)}, u32[]{:S(2)}, u32[]{:S(2)}) async-start(bf16[4,64,1536]{2,1,0:T(8,128)(2,1)} %broadcast_in_dim.15), calls=%async_computation | async-start | bytes 1572864 | tf_op jit(solution)/shard_map/all_to_all | solution.py:100
  16.4 5.1 %collective-permute-start.2 = (bf16[64,1536]{1,0:T(8,128)(2,1)}, bf16[64,1536]{1,0:T(8,128)(2,1)}, u32[]{:S(2)}, u32[]{:S(2)}) collective-permute-start(bf16[64,1536]{1,0:T(8,128)(2,1)} %pad_maximum_fusion.7), channel_id=1, source_target_pairs={{0,8},{1,9},{2,10},{3,11},{4,12},{5,13},{6,14},{7,15},{8,0},{9,1},... | collective-permute-start | bytes 589832 | tf_op jit(solution)/shard_map/ppermute | solution.py:56
  26.4 6.9 %collective-permute-done.2 = bf16[64,1536]{1,0:T(8,128)(2,1)} collective-permute-done((bf16[64,1536]{1,0:T(8,128)(2,1)}, bf16[64,1536]{1,0:T(8,128)(2,1)}, u32[]{:S(2)}, u32[]{:S(2)}) %collective-permute-start.2) | collective-permute-done | bytes 196640 | tf_op jit(solution)/shard_map/ppermute | solution.py:56
  33.4 6.9 %collective-permute-done.1 = bf16[64,1536]{1,0:T(8,128)(2,1)} collective-permute-done((bf16[64,1536]{1,0:T(8,128)(2,1)}, bf16[64,1536]{1,0:T(8,128)(2,1)}, u32[]{:S(2)}, u32[]{:S(2)}) %collective-permute-start.1) | collective-permute-done | bytes 196640 | tf_op jit(solution)/shard_map/ppermute | solution.py:56
  46.7 3.3 %collective-permute-start.6 = (bf16[4,64,1536]{2,1,0:T(8,128)(2,1)}, bf16[4,64,1536]{2,1,0:T(8,128)(2,1)}, u32[]{:S(2)}, u32[]{:S(2)}) collective-permute-start(bf16[4,64,1536]{2,1,0:T(8,128)(2,1)} %fusion.54), channel_id=1, source_target_pairs={{0,12},{1,13},{2,14},{3,15},{4,0},{5,1},{6,2},{7,3},{8,4},{9,5},{1... | collective-permute-start | bytes 2359304 | tf_op jit(solution)/shard_map/ppermute | solution.py:56
  55.0 5.8 %collective-permute-done.8 = bf16[256,1536]{1,0:T(8,128)(2,1)S(1)} collective-permute-done((bf16[256,1536]{1,0:T(8,128)(2,1)S(1)}, bf16[256,1536]{1,0:T(8,128)(2,1)S(1)}, u32[]{:S(2)}, u32[]{:S(2)}) %collective-permute-start.8) | collective-permute-done | bytes 786464 | tf_op jit(solution)/shard_map/ppermute | solution.py:56
  69.7 4.0 %all-to-all-start.1 = ((bf16[4,3,64,768]{3,2,1,0:T(8,128)(2,1)}), bf16[4,3,64,768]{3,2,1,0:T(8,128)(2,1)S(1)}, u32[]{:S(2)}, u32[]{:S(2)}) async-start(bf16[4,3,64,768]{3,2,1,0:T(8,128)(2,1)} %pad_maximum_fusion.2), calls=%async_computation.1 | async-start | bytes 2359296 | tf_op jit(solution)/shard_map/all_to_all | solution.py:80
  73.7 3.5 %convolution_convert_fusion.10 = bf16[256,768]{1,0:T(8,128)(2,1)} fusion(bf16[256,1536]{1,0:T(8,128)(2,1)} %bitcast.6, bf16[768,1536]{1,0:T(8,128)(2,1)} %copy-done.21), kind=kOutput, calls=%fused_computation.63 | convolution fusion | flops 604176384 | bytes 3538944 | tf_op jit(solution)/shard_map/dot_general | solution.py:60
  81.7 6.0 %all-to-all-done.1 = bf16[4,3,64,768]{3,2,1,0:T(8,128)(2,1)S(1)} async-done(((bf16[4,3,64,768]{3,2,1,0:T(8,128)(2,1)}), bf16[4,3,64,768]{3,2,1,0:T(8,128)(2,1)S(1)}, u32[]{:S(2)}, u32[]{:S(2)}) %all-to-all-start.1) | async-done | bytes 1179680 | tf_op jit(solution)/shard_map/all_to_all | solution.py:80
  88.3 3.5 %all-to-all-start.2 = ((bf16[4,1,64,768]{3,2,1,0:T(8,128)(2,1)}), bf16[4,1,64,768]{3,2,1,0:T(8,128)(2,1)S(1)}, u32[]{:S(2)}, u32[]{:S(2)}) async-start(bf16[4,1,64,768]{3,2,1,0:T(8,128)(2,1)} %bitcast.21), calls=%async_computation.2 | async-start | bytes 786432 | tf_op jit(solution)/shard_map/all_to_all | solution.py:80
  95.8 3.6 %collective-permute-start.12 = (bf16[2,64,1536]{2,1,0:T(8,128)(2,1)S(1)}, bf16[2,64,1536]{2,1,0:T(8,128)(2,1)}, u32[]{:S(2)}, u32[]{:S(2)}) collective-permute-start(bf16[2,64,1536]{2,1,0:T(8,128)(2,1)S(1)} %slice.148), channel_id=1, source_target_pairs={{0,12},{1,13},{2,14},{3,15},{4,0},{5,1},{6,2},{7,3},{8,4},{9,5},{1... | collective-permute-start | bytes 1179656 | tf_op jit(solution)/shard_map/ppermute | solution.py:56
  101.3 4.2 %all-to-all-start.3 = ((bf16[4,4,64,768]{3,2,1,0:T(8,128)(2,1)}), bf16[4,4,64,768]{3,2,1,0:T(8,128)(2,1)S(1)}, u32[]{:S(2)}, u32[]{:S(2)}) async-start(bf16[4,4,64,768]{3,2,1,0:T(8,128)(2,1)} %broadcast_in_dim.16), calls=%async_computation.3 | async-start | bytes 3145728 | tf_op jit(solution)/shard_map/all_to_all | solution.py:80
  115.4 6.0 %all-to-all-done.3 = bf16[4,4,64,768]{3,2,1,0:T(8,128)(2,1)S(1)} async-done(((bf16[4,4,64,768]{3,2,1,0:T(8,128)(2,1)}), bf16[4,4,64,768]{3,2,1,0:T(8,128)(2,1)S(1)}, u32[]{:S(2)}, u32[]{:S(2)}) %all-to-all-start.3) | async-done | bytes 1572896 | tf_op jit(solution)/shard_map/all_to_all | solution.py:80
  122.6 3.6 %all-to-all-start.4 = ((bf16[4,4,64,768]{3,2,1,0:T(8,128)(2,1)}), bf16[4,4,64,768]{3,2,1,0:T(8,128)(2,1)S(1)}, u32[]{:S(2)}, u32[]{:S(2)}) async-start(bf16[4,4,64,768]{3,2,1,0:T(8,128)(2,1)} %pad_maximum_fusion), calls=%async_computation.4 | async-start | bytes 3145728 | tf_op jit(solution)/shard_map/all_to_all | solution.py:80
  133.5 5.8 %collective-permute-start.14 = (bf16[768,768]{1,0:T(8,128)(2,1)}, bf16[768,768]{1,0:T(8,128)(2,1)}, u32[]{:S(2)}, u32[]{:S(2)}) collective-permute-start(bf16[768,768]{1,0:T(8,128)(2,1)} %fusion.46), channel_id=1, source_target_pairs={{0,16},{1,17},{2,18},{3,19},{4,20},{5,21},{6,22},{7,23},{8,24},{9,... | collective-permute-start | bytes 3538952 | tf_op jit(solution)/shard_map/ppermute | solution.py:56
  142.5 3.7 %all-to-all-start.5 = ((bf16[4,4,64,768]{3,2,1,0:T(8,128)(2,1)}), bf16[4,4,64,768]{3,2,1,0:T(8,128)(2,1)S(1)}, u32[]{:S(2)}, u32[]{:S(2)}) async-start(bf16[4,4,64,768]{3,2,1,0:T(8,128)(2,1)} %broadcast_in_dim.17), calls=%async_computation.5 | async-start | bytes 3145728 | tf_op jit(solution)/shard_map/all_to_all | solution.py:80
  152.9 6.7 %all-to-all-done.5 = bf16[4,4,64,768]{3,2,1,0:T(8,128)(2,1)S(1)} async-done(((bf16[4,4,64,768]{3,2,1,0:T(8,128)(2,1)}), bf16[4,4,64,768]{3,2,1,0:T(8,128)(2,1)S(1)}, u32[]{:S(2)}, u32[]{:S(2)}) %all-to-all-start.5) | async-done | bytes 1572896 | tf_op jit(solution)/shard_map/all_to_all | solution.py:80
  168.6 5.0 %collective-permute-done.22 = bf16[768,768]{1,0:T(8,128)(2,1)} collective-permute-done((bf16[768,768]{1,0:T(8,128)(2,1)S(1)}, bf16[768,768]{1,0:T(8,128)(2,1)}, u32[]{:S(2)}, u32[]{:S(2)}) %collective-permute-start.22) | collective-permute-done | bytes 1179680 | tf_op jit(solution)/shard_map/ppermute | solution.py:56
  175.0 8.0 %collective-permute-start.23 = (bf16[784,768]{1,0:T(8,128)(2,1)S(1)}, bf16[784,768]{1,0:T(8,128)(2,1)S(1)}, u32[]{:S(2)}, u32[]{:S(2)}) collective-permute-start(bf16[784,768]{1,0:T(8,128)(2,1)S(1)} %fusion.43), channel_id=1, source_target_pairs={{0,16},{1,17},{2,18},{3,19},{4,20},{5,21},{6,22},{7,23},{8,24},{9,... | collective-permute-start | bytes 3612680 | tf_op jit(solution)/shard_map/ppermute | solution.py:56
  183.0 16.1 %collective-permute-done.16 = bf16[256,1536]{1,0:T(8,128)(2,1)S(1)} collective-permute-done((bf16[256,1536]{1,0:T(8,128)(2,1)S(1)}, bf16[256,1536]{1,0:T(8,128)(2,1)S(1)}, u32[]{:S(2)}, u32[]{:S(2)}) %collective-permute-start.16) | collective-permute-done | bytes 786464 | tf_op jit(solution)/shard_map/ppermute | solution.py:56
  207.7 9.6 %collective-permute-done.20 = bf16[64,1536]{1,0:T(8,128)(2,1)} collective-permute-done((bf16[64,1536]{1,0:T(8,128)(2,1)}, bf16[64,1536]{1,0:T(8,128)(2,1)}, u32[]{:S(2)}, u32[]{:S(2)}) %collective-permute-start.20) | collective-permute-done | bytes 196640 | tf_op jit(solution)/shard_map/ppermute | solution.py:56
  219.6 5.8 %collective-permute-start.21 = (bf16[64,768]{1,0:T(8,128)(2,1)S(1)}, bf16[64,768]{1,0:T(8,128)(2,1)S(1)}, u32[]{:S(2)}, u32[]{:S(2)}) collective-permute-start(bf16[64,768]{1,0:T(8,128)(2,1)S(1)} %slice.210), channel_id=1, source_target_pairs={{0,16},{1,17},{2,18},{3,19},{4,20},{5,21},{6,22},{7,23},{8,24},{9,... | collective-permute-start | bytes 294920 | tf_op jit(solution)/shard_map/ppermute | solution.py:56
  229.1 14.5 %collective-permute-done.24 = bf16[784,768]{1,0:T(8,128)(2,1)} collective-permute-done((bf16[784,768]{1,0:T(8,128)(2,1)}, bf16[784,768]{1,0:T(8,128)(2,1)}, u32[]{:S(2)}, u32[]{:S(2)}) %collective-permute-start.24) | collective-permute-done | bytes 1204256 | tf_op jit(solution)/shard_map/ppermute | solution.py:56
  (183 shorter events, 101.0 us)
Async XLA Ops:
  8.2 38.5 %collective-permute-start.4 = (bf16[768,768]{1,0:T(8,128)(2,1)}, bf16[768,768]{1,0:T(8,128)(2,1)}, u32[]{:S(2)}, u32[]{:S(2)}) collective-permute-start(bf16[768,768]{1,0:T(8,128)(2,1)} %param.9), channel_id=1, source_target_pairs={{0,16},{1,17},{2,18},{3,19},{4,20},{5,21},{6,22},{7,23},{8,24},{9,... | collective-permute-start | bytes 3538952 | tf_op jit(solution)/shard_map/ppermute | solution.py:56
  8.3 38.4 %collective-permute-start.5 = (bf16[768,768]{1,0:T(8,128)(2,1)}, bf16[768,768]{1,0:T(8,128)(2,1)}, u32[]{:S(2)}, u32[]{:S(2)}) collective-permute-start(bf16[768,768]{1,0:T(8,128)(2,1)} %param.11), channel_id=1, source_target_pairs={{0,16},{1,17},{2,18},{3,19},{4,20},{5,21},{6,22},{7,23},{8,24},{9,... | collective-permute-start | bytes 3538952 | tf_op jit(solution)/shard_map/ppermute | solution.py:56
  10.2 31.3 %all-to-all-start = ((bf16[4,64,1536]{2,1,0:T(8,128)(2,1)}), bf16[4,64,1536]{2,1,0:T(8,128)(2,1)}, u32[]{:S(2)}, u32[]{:S(2)}) async-start(bf16[4,64,1536]{2,1,0:T(8,128)(2,1)} %broadcast_in_dim.15), calls=%async_computation | async-start | bytes 1572864 | tf_op jit(solution)/shard_map/all_to_all | solution.py:100
  16.4 17.0 %collective-permute-start.2 = (bf16[64,1536]{1,0:T(8,128)(2,1)}, bf16[64,1536]{1,0:T(8,128)(2,1)}, u32[]{:S(2)}, u32[]{:S(2)}) collective-permute-start(bf16[64,1536]{1,0:T(8,128)(2,1)} %pad_maximum_fusion.7), channel_id=1, source_target_pairs={{0,8},{1,9},{2,10},{3,11},{4,12},{5,13},{6,14},{7,15},{8,0},{9,1},... | collective-permute-start | bytes 589832 | tf_op jit(solution)/shard_map/ppermute | solution.py:56
  21.5 18.8 %collective-permute-start.1 = (bf16[64,1536]{1,0:T(8,128)(2,1)}, bf16[64,1536]{1,0:T(8,128)(2,1)}, u32[]{:S(2)}, u32[]{:S(2)}) collective-permute-start(bf16[64,1536]{1,0:T(8,128)(2,1)} %pad_maximum_fusion.7), channel_id=1, source_target_pairs={{0,12},{1,13},{2,14},{3,15},{4,0},{5,1},{6,2},{7,3},{8,4},{9,5},{1... | collective-permute-start | bytes 589832 | tf_op jit(solution)/shard_map/ppermute | solution.py:56
  41.5 19.2 %collective-permute-start.8 = (bf16[256,1536]{1,0:T(8,128)(2,1)S(1)}, bf16[256,1536]{1,0:T(8,128)(2,1)S(1)}, u32[]{:S(2)}, u32[]{:S(2)}) collective-permute-start(bf16[256,1536]{1,0:T(8,128)(2,1)S(1)} %pad_maximum_fusion.3), channel_id=1, source_target_pairs={{0,3},{1,0},{2,1},{3,2},{4,7},{5,4},{6,5},{7,6},{8,11},{9,8},{10,9... | collective-permute-start | bytes 2359304 | tf_op jit(solution)/shard_map/ppermute | solution.py:56
  44.3 19.5 %collective-permute-start.9 = (bf16[256,1536]{1,0:T(8,128)(2,1)S(1)}, bf16[256,1536]{1,0:T(8,128)(2,1)S(1)}, u32[]{:S(2)}, u32[]{:S(2)}) collective-permute-start(bf16[256,1536]{1,0:T(8,128)(2,1)S(1)} %pad_maximum_fusion.3), channel_id=1, source_target_pairs={{0,1},{1,2},{2,3},{3,0},{4,5},{5,6},{6,7},{7,4},{8,9},{9,10},{10,1... | collective-permute-start | bytes 2359304 | tf_op jit(solution)/shard_map/ppermute | solution.py:56
  46.7 47.0 %collective-permute-start.6 = (bf16[4,64,1536]{2,1,0:T(8,128)(2,1)}, bf16[4,64,1536]{2,1,0:T(8,128)(2,1)}, u32[]{:S(2)}, u32[]{:S(2)}) collective-permute-start(bf16[4,64,1536]{2,1,0:T(8,128)(2,1)} %fusion.54), channel_id=1, source_target_pairs={{0,12},{1,13},{2,14},{3,15},{4,0},{5,1},{6,2},{7,3},{8,4},{9,5},{1... | collective-permute-start | bytes 2359304 | tf_op jit(solution)/shard_map/ppermute | solution.py:56
  49.9 43.8 %collective-permute-start.7 = (bf16[4,64,1536]{2,1,0:T(8,128)(2,1)}, bf16[4,64,1536]{2,1,0:T(8,128)(2,1)}, u32[]{:S(2)}, u32[]{:S(2)}) collective-permute-start(bf16[4,64,1536]{2,1,0:T(8,128)(2,1)} %fusion.54), channel_id=1, source_target_pairs={{0,4},{1,5},{2,6},{3,7},{4,8},{5,9},{6,10},{7,11},{8,12},{9,13},{1... | collective-permute-start | bytes 2359304 | tf_op jit(solution)/shard_map/ppermute | solution.py:56
  69.7 18.0 %all-to-all-start.1 = ((bf16[4,3,64,768]{3,2,1,0:T(8,128)(2,1)}), bf16[4,3,64,768]{3,2,1,0:T(8,128)(2,1)S(1)}, u32[]{:S(2)}, u32[]{:S(2)}) async-start(bf16[4,3,64,768]{3,2,1,0:T(8,128)(2,1)} %pad_maximum_fusion.2), calls=%async_computation.1 | async-start | bytes 2359296 | tf_op jit(solution)/shard_map/all_to_all | solution.py:80
  94.7 15.6 %collective-permute-start.13 = (bf16[2,64,1536]{2,1,0:T(8,128)(2,1)S(1)}, bf16[2,64,1536]{2,1,0:T(8,128)(2,1)}, u32[]{:S(2)}, u32[]{:S(2)}) collective-permute-start(bf16[2,64,1536]{2,1,0:T(8,128)(2,1)S(1)} %slice.149), channel_id=1, source_target_pairs={{0,4},{1,5},{2,6},{3,7},{4,8},{5,9},{6,10},{7,11},{8,12},{9,13},{1... | collective-permute-start | bytes 1179656 | tf_op jit(solution)/shard_map/ppermute | solution.py:56
  95.8 16.1 %collective-permute-start.12 = (bf16[2,64,1536]{2,1,0:T(8,128)(2,1)S(1)}, bf16[2,64,1536]{2,1,0:T(8,128)(2,1)}, u32[]{:S(2)}, u32[]{:S(2)}) collective-permute-start(bf16[2,64,1536]{2,1,0:T(8,128)(2,1)S(1)} %slice.148), channel_id=1, source_target_pairs={{0,12},{1,13},{2,14},{3,15},{4,0},{5,1},{6,2},{7,3},{8,4},{9,5},{1... | collective-permute-start | bytes 1179656 | tf_op jit(solution)/shard_map/ppermute | solution.py:56
  101.3 20.1 %all-to-all-start.3 = ((bf16[4,4,64,768]{3,2,1,0:T(8,128)(2,1)}), bf16[4,4,64,768]{3,2,1,0:T(8,128)(2,1)S(1)}, u32[]{:S(2)}, u32[]{:S(2)}) async-start(bf16[4,4,64,768]{3,2,1,0:T(8,128)(2,1)} %broadcast_in_dim.16), calls=%async_computation.3 | async-start | bytes 3145728 | tf_op jit(solution)/shard_map/all_to_all | solution.py:80
  122.6 18.2 %all-to-all-start.4 = ((bf16[4,4,64,768]{3,2,1,0:T(8,128)(2,1)}), bf16[4,4,64,768]{3,2,1,0:T(8,128)(2,1)S(1)}, u32[]{:S(2)}, u32[]{:S(2)}) async-start(bf16[4,4,64,768]{3,2,1,0:T(8,128)(2,1)} %pad_maximum_fusion), calls=%async_computation.4 | async-start | bytes 3145728 | tf_op jit(solution)/shard_map/all_to_all | solution.py:80
  133.5 16.4 %collective-permute-start.14 = (bf16[768,768]{1,0:T(8,128)(2,1)}, bf16[768,768]{1,0:T(8,128)(2,1)}, u32[]{:S(2)}, u32[]{:S(2)}) collective-permute-start(bf16[768,768]{1,0:T(8,128)(2,1)} %fusion.46), channel_id=1, source_target_pairs={{0,16},{1,17},{2,18},{3,19},{4,20},{5,21},{6,22},{7,23},{8,24},{9,... | collective-permute-start | bytes 3538952 | tf_op jit(solution)/shard_map/ppermute | solution.py:56
  142.5 17.1 %all-to-all-start.5 = ((bf16[4,4,64,768]{3,2,1,0:T(8,128)(2,1)}), bf16[4,4,64,768]{3,2,1,0:T(8,128)(2,1)S(1)}, u32[]{:S(2)}, u32[]{:S(2)}) async-start(bf16[4,4,64,768]{3,2,1,0:T(8,128)(2,1)} %broadcast_in_dim.17), calls=%async_computation.5 | async-start | bytes 3145728 | tf_op jit(solution)/shard_map/all_to_all | solution.py:80
  152.8 20.7 %collective-permute-start.22 = (bf16[768,768]{1,0:T(8,128)(2,1)S(1)}, bf16[768,768]{1,0:T(8,128)(2,1)}, u32[]{:S(2)}, u32[]{:S(2)}) collective-permute-start(bf16[768,768]{1,0:T(8,128)(2,1)S(1)} %add_convert_fusion.1), channel_id=1, source_target_pairs={{0,128},{1,129},{2,130},{3,131},{4,132},{5,133},{6,134},{7,135},{8... | collective-permute-start | bytes 3538952 | tf_op jit(solution)/shard_map/ppermute | solution.py:56
  162.2 20.8 %collective-permute-start.17 = (bf16[256,1536]{1,0:T(8,128)(2,1)S(1)}, bf16[256,1536]{1,0:T(8,128)(2,1)S(1)}, u32[]{:S(2)}, u32[]{:S(2)}) collective-permute-start(bf16[256,1536]{1,0:T(8,128)(2,1)S(1)} %convolution_convert_fusion), channel_id=1, source_target_pairs={{0,2},{1,3},{2,0},{3,1},{4,6},{5,7},{6,4},{7,5},{8,10},{9,11},{10,... | collective-permute-start | bytes 2359304 | tf_op jit(solution)/shard_map/ppermute | solution.py:56
  166.1 33.0 %collective-permute-start.16 = (bf16[256,1536]{1,0:T(8,128)(2,1)S(1)}, bf16[256,1536]{1,0:T(8,128)(2,1)S(1)}, u32[]{:S(2)}, u32[]{:S(2)}) collective-permute-start(bf16[256,1536]{1,0:T(8,128)(2,1)S(1)} %convolution_convert_fusion.1), channel_id=1, source_target_pairs={{0,3},{1,0},{2,1},{3,2},{4,7},{5,4},{6,5},{7,6},{8,11},{9,8},{10,9... | collective-permute-start | bytes 2359304 | tf_op jit(solution)/shard_map/ppermute | solution.py:56
  167.8 31.3 %collective-permute-start.15 = (bf16[256,1536]{1,0:T(8,128)(2,1)S(1)}, bf16[256,1536]{1,0:T(8,128)(2,1)S(1)}, u32[]{:S(2)}, u32[]{:S(2)}) collective-permute-start(bf16[256,1536]{1,0:T(8,128)(2,1)S(1)} %convolution_convert_fusion.2), channel_id=1, source_target_pairs={{0,1},{1,2},{2,3},{3,0},{4,5},{5,6},{6,7},{7,4},{8,9},{9,10},{10,1... | collective-permute-start | bytes 2359304 | tf_op jit(solution)/shard_map/ppermute | solution.py:56
  175.0 30.1 %collective-permute-start.23 = (bf16[784,768]{1,0:T(8,128)(2,1)S(1)}, bf16[784,768]{1,0:T(8,128)(2,1)S(1)}, u32[]{:S(2)}, u32[]{:S(2)}) collective-permute-start(bf16[784,768]{1,0:T(8,128)(2,1)S(1)} %fusion.43), channel_id=1, source_target_pairs={{0,16},{1,17},{2,18},{3,19},{4,20},{5,21},{6,22},{7,23},{8,24},{9,... | collective-permute-start | bytes 3612680 | tf_op jit(solution)/shard_map/ppermute | solution.py:56
  200.9 16.4 %collective-permute-start.20 = (bf16[64,1536]{1,0:T(8,128)(2,1)}, bf16[64,1536]{1,0:T(8,128)(2,1)}, u32[]{:S(2)}, u32[]{:S(2)}) collective-permute-start(bf16[64,1536]{1,0:T(8,128)(2,1)} %get-tuple-element.39), channel_id=1, source_target_pairs={{0,12},{1,13},{2,14},{3,15},{4,0},{5,1},{6,2},{7,3},{8,4},{9,5},{1... | collective-permute-start | bytes 589832 | tf_op jit(solution)/shard_map/ppermute | solution.py:56
  203.0 15.4 %collective-permute-start.18 = (bf16[64,1536]{1,0:T(8,128)(2,1)}, bf16[64,1536]{1,0:T(8,128)(2,1)}, u32[]{:S(2)}, u32[]{:S(2)}) collective-permute-start(bf16[64,1536]{1,0:T(8,128)(2,1)} %get-tuple-element.38), channel_id=1, source_target_pairs={{0,4},{1,5},{2,6},{3,7},{4,8},{5,9},{6,10},{7,11},{8,12},{9,13},{1... | collective-permute-start | bytes 589832 | tf_op jit(solution)/shard_map/ppermute | solution.py:56
  207.7 35.9 %collective-permute-start.24 = (bf16[784,768]{1,0:T(8,128)(2,1)}, bf16[784,768]{1,0:T(8,128)(2,1)}, u32[]{:S(2)}, u32[]{:S(2)}) collective-permute-start(bf16[784,768]{1,0:T(8,128)(2,1)} %pad_maximum_fusion.1), channel_id=1, source_target_pairs={{0,128},{1,129},{2,130},{3,131},{4,132},{5,133},{6,134},{7,135},{8... | collective-permute-start | bytes 3612680 | tf_op jit(solution)/shard_map/ppermute | solution.py:56
  (42 other events, 300.8 us)
where the time goes:
time: 249 us; the launch traced here: 247 us
  waiting for transfers between devices  91.3 us (37%)
  starting transfers between devices  75.6 us (30%)
  local copies, waits for them, and re-layouts  33.6 us (13%)
  matrix products  24.6 us (10%)
  other arithmetic  20.9 us (8%)
    ppermute x25, waiting for transfers between devices, send(): return lax.ppermute(value, AXES, pairs)  71.1 us
    ppermute x25, starting transfers between devices, send(): return lax.ppermute(value, AXES, pairs)  52.4 us
    dot_general x16, matrix products, dot(): lax.dot_general(a, b, ((contract[:1], contract[1:]), ((), ())), preferred...  24.6 us
    all_to_all x5, waiting for transfers between devices, swap_x(): lax.all_to_all(value, 'row', 0, 0, tiled=True, axis_index_groups=X_SETS)  20.2 us
    all_to_all x5, starting transfers between devices, swap_x(): lax.all_to_all(value, 'row', 0, 0, tiled=True, axis_index_groups=X_SETS)  18.9 us
    unnamed x73, local copies, waits for them, and re-layouts  8.86 us
    slice x4, local copies, waits for them, and re-layouts, on_device(): c_mine = jnp.concatenate([c[:, :width] for c in cs])  6.7 us
  transfers between devices with their start and end apart: 31, of which 16 were waited for; matrix products, arithmetic and copies ran while one was open for 27% of the time, Pallas kernels for 0%

commit v1 on v0

--- a/solution.py
+++ b/solution.py
@@ -49,7 +49,6 @@
 X_SETS = [[c + 2 * x for x in range(4)] for c in range(2)]
 
 Y_SETS = [[z * 4 + y for y in range(4)] for z in range(4)]
-IN_GROUPS = ((0, 1, 3), (2,))
 
 
 def send(value, pairs):
@@ -73,9 +72,6 @@
     def after(value, *others):
         return lax.optimization_barrier((value, *others))[0]
 
-    def gather_z(value):
-        return jnp.concatenate([value] + [send(value, Z_BY[4 - j]) for j in range(1, 4)], axis=0)
-
     def swap_x(value):
         return lax.all_to_all(value, "row", 0, 0, tiled=True, axis_index_groups=X_SETS)
 
@@ -96,70 +92,71 @@
     w_in_all = jnp.concatenate([w_in, w_in_got], axis=0)
     w_out_all = jnp.concatenate([w_out, w_out_got], axis=1)
 
-    x_own = gather_z(x_half)
-    c_four = lax.all_to_all(
-        jnp.broadcast_to(c_half[None], (4,) + c_half.shape), "col", 0, 0, tiled=True, axis_index_groups=Y_SETS
-    )
+    x_one, x_three, x_two = (send(x_half, Z_BY[4 - j]) for j in (1, 3, 2))
+    c_four = jnp.broadcast_to(after(c_half, x_half)[None], (4,) + c_half.shape)
+    c_four = lax.all_to_all(c_four, "col", 0, 0, tiled=True, axis_index_groups=Y_SETS)
     y = lax.axis_index("col") % 4
     c_own = lax.dynamic_slice_in_dim(jnp.concatenate([c_four, c_four]), y, 4, 0)
+    x_own = jnp.concatenate([x_half, x_one, x_two, x_three])
 
-    x_own = after(x_own, c_four)
     x_up, x_down = send(x_own, Y_BY[3]), send(x_own, Y_BY[1])
     c_own = after(c_own, x_own, w_in_got, w_out_got)
     c_up, c_down = send(c_own, Z_BY[3]), send(c_own, Z_BY[1])
-    xs = [x_own, x_up, None, x_down]
     parts = [dot(x_own, w_in_all, (1, 0), bf), None, None, None]
     x_up, x_down = after((x_up, x_down), parts[0])
     rows = 2 * half
-    xs[1], xs[3] = x_up, x_down
-    xs[2] = jnp.concatenate([send(x_up[:rows], Y_BY[3]), send(x_down[rows:], Y_BY[1])])
-    acts, slopes = [None] * 4, [None] * 4
-    pre = None
-    for g in IN_GROUPS:
-        for k in g:
-            if parts[k] is None:
-                parts[k] = dot(xs[k], w_in_all, (1, 0), bf)
-        part = jnp.stack([parts[k].reshape(4, half, hidden) for k in g], axis=1)
-        pre = scatter_x(part if pre is None else after(part, pre)) + b_in[None, None, :]
-        act, slope = gelu_pair(pre)
-        for i, k in enumerate(g):
-            acts[k], slopes[k] = act[i], slope[i]
-    act_all = gather_x(jnp.stack(acts).astype(bf))
+    far = [send(x_up[:rows], Y_BY[3]), send(x_down[rows:], Y_BY[1])]
+    parts[1], parts[3] = dot(x_up, w_in_all, (1, 0), bf), dot(x_down, w_in_all, (1, 0), bf)
+    x_far = jnp.concatenate(after(far, parts[1], parts[3]))
+    parts[2] = dot(x_far, w_in_all, (1, 0), bf)
+    xs = [x_own, x_up, x_far, x_down]
+    parts = jnp.stack([part.reshape(4, half, hidden) for part in parts], axis=1)
 
-    c_up, c_down = after((c_up, c_down), parts[2])
+    c_up, c_down = after((c_up, c_down), parts)
     c_far = jnp.concatenate([send(c_up[:2], Z_BY[3]), send(c_down[2:], Z_BY[1])])
     cs = [c.reshape(-1, 2 * width) for c in (c_own, c_up, c_far, c_down)]
+
+    pre = scatter_x(parts) + b_in[None, None, :]
+    act, slope = gelu_pair(pre)
+    act_all = gather_x(act.astype(bf))
+
     d_parts = jnp.stack([dot(c, w_out_all, (1, 1), bf).reshape(4, half, hidden) for c in cs])
-    d_act = scatter_x(after(d_parts, act_all))
-    d_pre_all = gather_x((d_act * jnp.stack(slopes)).astype(bf))
+    c_mine = jnp.concatenate([c[:, :width] for c in cs])
+    c_other = jnp.concatenate([c[:, width:] for c in cs])
+    act_all = after(act_all, c_mine, c_other, d_parts)
+    d_act = swap_x(after(d_parts, act_all))
 
     act_all = act_all.reshape(-1, hidden)
-    c_mine = jnp.concatenate([c[:, :width] for c in cs])
-    c_other = jnp.concatenate([c[:, width:] for c in cs])
     out_got = send(dot(act_all, c_other, (0, 0), bf), CORE)
     out_mine = (dot(act_all, c_mine, (0, 0)) + out_got.astype(f32)).astype(bf)
     out_deep = send(out_mine, DEPTH)
     d_w_out = out_mine.astype(f32) + out_deep.astype(f32)
 
-    d_pre_all = after(d_pre_all, out_mine).swapaxes(0, 1)
-    d_pres = [d_pre_all[k].reshape(4 * half, hidden) for k in range(4)]
-    shares = [dot(d_pres[k], w_in_all, (1, 1), bf) for k in (1, 3, 2)]
-    d_pre_all = after(d_pre_all, out_deep, *shares)
-    d_pre_rows = d_pre_all.reshape(-1, hidden)
+    d_act = jnp.sum(after(d_act, out_mine).astype(f32), axis=0)
+    d_pre_all = gather_x((d_act * slope).astype(bf))
+
     x_mine = jnp.concatenate([x[:, :width] for x in xs])
     x_other = jnp.concatenate([x[:, width:] for x in xs])
     x_other = jnp.concatenate([x_other, jnp.ones((x_other.shape[0], 16), bf)], axis=1)
-    in_other = dot(x_other, d_pre_rows, (0, 0), bf)
+    d_pre_all = after(d_pre_all, x_mine, x_other).swapaxes(0, 1)
+    d_pre_rows = d_pre_all.reshape(-1, hidden)
+    in_other = dot(x_other, after(d_pre_rows, out_deep), (0, 0), bf)
     in_got = send(in_other, CORE)
+    d_pres = [d_pre_rows[4 * half * k : 4 * half * (k + 1)] for k in range(4)]
+    d_pres = after(d_pres, in_other)
+    shares = [dot(d_pres[k], w_in_all, (1, 1), bf) for k in (1, 3, 2)]
+    got = [send(share, Y_BY[k]) for share, k in zip(shares, (1, 3, 2))]
+    in_got = after(in_got, *shares)
     in_mine = (dot(x_mine, d_pre_rows, (0, 0)) + in_got[:width].astype(f32)).astype(bf)
     bias = (in_other[width:].astype(f32) + in_got[width:].astype(f32)).astype(bf)
-    in_mine = jnp.concatenate([in_mine, bias])
-    d_in = in_mine.astype(f32) + send(in_mine, DEPTH).astype(f32)
-    d_w_in, d_b_in = d_in[:width], d_in[width]
+    in_both = jnp.concatenate([in_mine, bias])
+    in_deep = send(in_both, DEPTH)
+    d_w_in = in_mine.astype(f32) + in_deep[:width].astype(f32)
+    d_b_in = bias[0].astype(f32) + in_deep[width].astype(f32)
 
     total = dot(d_pres[0], w_in_all, (1, 1))
-    for k, share in zip((1, 3, 2), shares):
-        total = total + send(share, Y_BY[k]).astype(f32)
+    for term in after(got, in_both):
+        total = total + term.astype(f32)
     total = total.reshape(4, half, 2 * width)
     d_half = total[0]
     for j in range(1, 4):

time: 249 us -> 286 us (1.15)
  waiting for transfers between devices: 91.3 us -> 135 us
  starting transfers between devices: 75.6 us -> 64.2 us
  matrix products: 24.6 us -> 31.6 us
  local copies, waits for them, and re-layouts: 33.6 us -> 27.8 us
    all_to_all x5 -> x4, waiting for transfers between devices: 20.2 us -> 42.3 us  [swap_x(): lax.all_to_all(value, 'row', 0, 0, tiled=True, axis_index_groups=X_SETS)]
    ppermute x25, waiting for transfers between devices: 71.1 us -> 92.3 us  [send(): return lax.ppermute(value, AXES, pairs)]
    ppermute x25, starting transfers between devices: 52.4 us -> 44.5 us  [send(): return lax.ppermute(value, AXES, pairs)]
    dot_general x16, matrix products: 24.6 us -> 31.6 us  [dot(): lax.dot_general(a, b, ((contract[:1], contract[1:]), ((), ())), preferred...]
    unnamed x73 -> x61, local copies, waits for them, and re-layouts: 8.86 us -> 3.27 us
    all_to_all x5 -> x4, starting transfers between devices: 18.9 us -> 15.5 us  [swap_x(): lax.all_to_all(value, 'row', 0, 0, tiled=True, axis_index_groups=X_SETS)]
  transfers between devices with their start and end apart: 31 -> 30, of which waited for: 16 -> 16; matrix products, arithmetic and copies ran while one was open for 27% -> 22% of each run, Pallas kernels for 0% -> 0%
where the time goes in v1:
time: 286 us; the launch traced here: 283 us
  waiting for transfers between devices  135 us (47%)
  starting transfers between devices  64.2 us (22%)
  matrix products  31.6 us (11%)
  local copies, waits for them, and re-layouts  27.8 us (10%)
  other arithmetic  23.7 us (8%)
    ppermute x25, waiting for transfers between devices, send(): return lax.ppermute(value, AXES, pairs)  92.3 us
    ppermute x25, starting transfers between devices, send(): return lax.ppermute(value, AXES, pairs)  44.5 us
    all_to_all x4, waiting for transfers between devices, swap_x(): lax.all_to_all(value, 'row', 0, 0, tiled=True, axis_index_groups=X_SETS)  42.3 us
    dot_general x16, matrix products, dot(): lax.dot_general(a, b, ((contract[:1], contract[1:]), ((), ())), preferred...  31.6 us
    all_to_all x4, starting transfers between devices, swap_x(): lax.all_to_all(value, 'row', 0, 0, tiled=True, axis_index_groups=X_SETS)  15.5 us
    slice x4, local copies, waits for them, and re-layouts, on_device(): c_mine = jnp.concatenate([c[:, :width] for c in cs])  7.34 us
  transfers between devices with their start and end apart: 30, of which 16 were waited for; matrix products, arithmetic and copies ran while one was open for 22% of the time, Pallas kernels for 0%

profile of v1, /device:TPU:1, one launch (start us, length us, event | category | flops | bytes accessed | tf_op | source)
XLA Modules:
  0.0 283.3 jit_solution(17302731466732013169)
XLA Ops:
  4.8 3.3 %collective-permute-start = (bf16[2,64,768]{2,1,0:T(8,128)(2,1)S(1)}, bf16[2,64,768]{2,1,0:T(8,128)(2,1)S(1)}, u32[]{:S(2)}, u32[]{:S(2)}) collective-permute-start(bf16[2,64,768]{2,1,0:T(8,128)(2,1)S(1)} %get-tuple-element.72), channel_id=1, source_target_pairs={{0,16},{1,17},{2,18},{3,19},{4,20},{5,21},{6,22},{7,23},{8,24},{9,... | collective-permute-start | bytes 589832 | tf_op jit(solution)/shard_map/ppermute | solution.py:55
  11.3 5.1 %collective-permute-start.2 = (bf16[64,1536]{1,0:T(8,128)(2,1)}, bf16[64,1536]{1,0:T(8,128)(2,1)}, u32[]{:S(2)}, u32[]{:S(2)}) collective-permute-start(bf16[64,1536]{1,0:T(8,128)(2,1)} %pad_maximum_fusion.9), channel_id=1, source_target_pairs={{0,8},{1,9},{2,10},{3,11},{4,12},{5,13},{6,14},{7,15},{8,0},{9,1},... | collective-permute-start | bytes 589832 | tf_op jit(solution)/shard_map/ppermute | solution.py:55
  19.7 4.2 %all-to-all-start = ((bf16[4,64,1536]{2,1,0:T(8,128)(2,1)}), bf16[4,64,1536]{2,1,0:T(8,128)(2,1)}, u32[]{:S(2)}, u32[]{:S(2)}) async-start(bf16[4,64,1536]{2,1,0:T(8,128)(2,1)} %broadcast_in_dim.15), calls=%async_computation | async-start | bytes 1572864 | tf_op jit(solution)/shard_map/all_to_all | solution.py:97
  24.1 4.5 %collective-permute-done.2 = bf16[64,1536]{1,0:T(8,128)(2,1)} collective-permute-done((bf16[64,1536]{1,0:T(8,128)(2,1)}, bf16[64,1536]{1,0:T(8,128)(2,1)}, u32[]{:S(2)}, u32[]{:S(2)}) %collective-permute-start.2) | collective-permute-done | bytes 196640 | tf_op jit(solution)/shard_map/ppermute | solution.py:55
  28.6 6.7 %collective-permute-done.1 = bf16[64,1536]{1,0:T(8,128)(2,1)} collective-permute-done((bf16[64,1536]{1,0:T(8,128)(2,1)}, bf16[64,1536]{1,0:T(8,128)(2,1)}, u32[]{:S(2)}, u32[]{:S(2)}) %collective-permute-start.1) | collective-permute-done | bytes 196640 | tf_op jit(solution)/shard_map/ppermute | solution.py:55
  42.7 3.4 %collective-permute-start.6 = (bf16[4,64,1536]{2,1,0:T(8,128)(2,1)}, bf16[4,64,1536]{2,1,0:T(8,128)(2,1)}, u32[]{:S(2)}, u32[]{:S(2)}) collective-permute-start(bf16[4,64,1536]{2,1,0:T(8,128)(2,1)} %fusion.16), channel_id=1, source_target_pairs={{0,12},{1,13},{2,14},{3,15},{4,0},{5,1},{6,2},{7,3},{8,4},{9,5},{1... | collective-permute-start | bytes 2359304 | tf_op jit(solution)/shard_map/ppermute | solution.py:55
  50.0 5.7 %collective-permute-done.8 = bf16[256,1536]{1,0:T(8,128)(2,1)} collective-permute-done((bf16[256,1536]{1,0:T(8,128)(2,1)S(1)}, bf16[256,1536]{1,0:T(8,128)(2,1)}, u32[]{:S(2)}, u32[]{:S(2)}) %collective-permute-start.8) | collective-permute-done | bytes 786464 | tf_op jit(solution)/shard_map/ppermute | solution.py:55
  76.1 4.0 %all-to-all-start.1 = ((bf16[4,4,64,768]{3,2,1,0:T(8,128)(2,1)}), bf16[4,4,64,768]{3,2,1,0:T(8,128)(2,1)S(1)}, u32[]{:S(2)}, u32[]{:S(2)}) async-start(bf16[4,4,64,768]{3,2,1,0:T(8,128)(2,1)} %pad_maximum_fusion), calls=%async_computation.1 | async-start | bytes 3145728 | tf_op jit(solution)/shard_map/all_to_all | solution.py:76
  100.1 4.4 %all-to-all-start.2 = ((bf16[4,4,64,768]{3,2,1,0:T(8,128)(2,1)}), bf16[4,4,64,768]{3,2,1,0:T(8,128)(2,1)}, u32[]{:S(2)}, u32[]{:S(2)}) async-start(bf16[4,4,64,768]{3,2,1,0:T(8,128)(2,1)} %broadcast_in_dim.16), calls=%async_computation.2 | async-start | bytes 3145728 | tf_op jit(solution)/shard_map/all_to_all | solution.py:76
  111.3 10.4 %all-to-all-done.2 = bf16[4,4,64,768]{3,2,1,0:T(8,128)(2,1)} async-done(((bf16[4,4,64,768]{3,2,1,0:T(8,128)(2,1)}), bf16[4,4,64,768]{3,2,1,0:T(8,128)(2,1)}, u32[]{:S(2)}, u32[]{:S(2)}) %all-to-all-start.2) | async-done | bytes 1572896 | tf_op jit(solution)/shard_map/all_to_all | solution.py:76
  121.7 4.0 %convolution_convert_fusion.4 = bf16[768,768]{1,0:T(8,128)(2,1)} fusion(bf16[1024,768]{1,0:T(8,128)(2,1)} %bitcast.22, bf16[256,768]{1,0:T(8,128)(2,1)S(1)} %copy-done.25, bf16[256,768]{1,0:T(8,128)(2,1)} %get-tuple-element.68, bf16[256,768]{1,0:T(8,128)(2,1)S(1)} %copy-done.26, bf16[256,768]{1,0:T(8,128)(2,1)S(1)} %copy-done.22), kind=kOutput, calls=%fused_computation.28 | convolution fusion | flops 1214840832 | bytes 4325376 | tf_op jit(solution)/shard_map/dot_general | solution.py:59
  125.6 4.5 %collective-permute-start.14 = (bf16[768,768]{1,0:T(8,128)(2,1)}, bf16[768,768]{1,0:T(8,128)(2,1)}, u32[]{:S(2)}, u32[]{:S(2)}) collective-permute-start(bf16[768,768]{1,0:T(8,128)(2,1)} %convolution_convert_fusion.4), channel_id=1, source_target_pairs={{0,16},{1,17},{2,18},{3,19},{4,20},{5,21},{6,22},{7,23},{8,24},{9,... | collective-permute-start | bytes 3538952 | tf_op jit(solution)/shard_map/ppermute | solution.py:55
  130.1 3.6 %all-to-all-start.3 = ((bf16[4,4,64,768]{3,2,1,0:T(8,128)(2,1)}), bf16[4,4,64,768]{3,2,1,0:T(8,128)(2,1)S(1)}, u32[]{:S(2)}, u32[]{:S(2)}) async-start(bf16[4,4,64,768]{3,2,1,0:T(8,128)(2,1)} %pad_maximum_fusion.1), calls=%async_computation.3 | async-start | bytes 3145728 | tf_op jit(solution)/shard_map/all_to_all | solution.py:76
  133.7 4.6 %add_convert_fusion.1 = bf16[768,768]{1,0:T(8,128)(2,1)} fusion(bf16[768,768]{1,0:T(8,128)(2,1)} %collective-permute-done.14, bf16[1024,768]{1,0:T(8,128)(2,1)} %bitcast.22, bf16[256,768]{1,0:T(8,128)(2,1)} %get-tuple-element.69, bf16[256,768]{1,0:T(8,128)(2,1)} %get-tuple-element.67, bf16[256,768]{1,0:T(8,128)(2,1)} %get-tuple-element.65, ...), kind=kOutput, calls=%fused_computation.16 | convolution fusion | flops 1216020480 | bytes 5505024 | tf_op jit(solution)/shard_map/dot_general | solution.py:59
  138.3 16.1 %all-to-all-done.3 = bf16[4,4,64,768]{3,2,1,0:T(8,128)(2,1)S(1)} async-done(((bf16[4,4,64,768]{3,2,1,0:T(8,128)(2,1)}), bf16[4,4,64,768]{3,2,1,0:T(8,128)(2,1)S(1)}, u32[]{:S(2)}, u32[]{:S(2)}) %all-to-all-start.3) | async-done | bytes 1572896 | tf_op jit(solution)/shard_map/all_to_all | solution.py:76
  156.5 3.6 %all-to-all-start.4 = ((bf16[4,4,64,768]{3,2,1,0:T(8,128)(2,1)}), bf16[4,4,64,768]{3,2,1,0:T(8,128)(2,1)S(1)}, u32[]{:S(2)}, u32[]{:S(2)}) async-start(bf16[4,4,64,768]{3,2,1,0:T(8,128)(2,1)} %broadcast_in_dim.17), calls=%async_computation.4 | async-start | bytes 3145728 | tf_op jit(solution)/shard_map/all_to_all | solution.py:76
  164.5 15.3 %all-to-all-done.4 = bf16[4,4,64,768]{3,2,1,0:T(8,128)(2,1)S(1)} async-done(((bf16[4,4,64,768]{3,2,1,0:T(8,128)(2,1)}), bf16[4,4,64,768]{3,2,1,0:T(8,128)(2,1)S(1)}, u32[]{:S(2)}, u32[]{:S(2)}) %all-to-all-start.4) | async-done | bytes 1572896 | tf_op jit(solution)/shard_map/all_to_all | solution.py:76
  179.9 7.3 %collective-permute-done.15 = bf16[768,768]{1,0:T(8,128)(2,1)} collective-permute-done((bf16[768,768]{1,0:T(8,128)(2,1)}, bf16[768,768]{1,0:T(8,128)(2,1)}, u32[]{:S(2)}, u32[]{:S(2)}) %collective-permute-start.15) | collective-permute-done | bytes 1179680 | tf_op jit(solution)/shard_map/ppermute | solution.py:55
  200.4 30.0 %collective-permute-done.16 = bf16[256,1536]{1,0:T(8,128)(2,1)S(1)} collective-permute-done((bf16[256,1536]{1,0:T(8,128)(2,1)S(1)}, bf16[256,1536]{1,0:T(8,128)(2,1)S(1)}, u32[]{:S(2)}, u32[]{:S(2)}) %collective-permute-start.16) | collective-permute-done | bytes 786464 | tf_op jit(solution)/shard_map/ppermute | solution.py:55
  232.1 3.3 %collective-permute-start.22 = (bf16[64,1536]{1,0:T(8,128)(2,1)}, bf16[64,1536]{1,0:T(8,128)(2,1)S(1)}, u32[]{:S(2)}, u32[]{:S(2)}) collective-permute-start(bf16[64,1536]{1,0:T(8,128)(2,1)} %get-tuple-element.53), channel_id=1, source_target_pairs={{0,12},{1,13},{2,14},{3,15},{4,0},{5,1},{6,2},{7,3},{8,4},{9,5},{1... | collective-permute-start | bytes 589832 | tf_op jit(solution)/shard_map/ppermute | solution.py:55
  237.5 11.8 %collective-permute-done.22 = bf16[64,1536]{1,0:T(8,128)(2,1)S(1)} collective-permute-done((bf16[64,1536]{1,0:T(8,128)(2,1)}, bf16[64,1536]{1,0:T(8,128)(2,1)S(1)}, u32[]{:S(2)}, u32[]{:S(2)}) %collective-permute-start.22) | collective-permute-done | bytes 196640 | tf_op jit(solution)/shard_map/ppermute | solution.py:55
  249.3 3.4 %collective-permute-done.20 = bf16[64,1536]{1,0:T(8,128)(2,1)} collective-permute-done((bf16[64,1536]{1,0:T(8,128)(2,1)S(1)}, bf16[64,1536]{1,0:T(8,128)(2,1)}, u32[]{:S(2)}, u32[]{:S(2)}) %collective-permute-start.20) | collective-permute-done | bytes 196640 | tf_op jit(solution)/shard_map/ppermute | solution.py:55
  253.7 5.6 %collective-permute-start.23 = (bf16[64,768]{1,0:T(8,128)(2,1)S(1)}, bf16[64,768]{1,0:T(8,128)(2,1)S(1)}, u32[]{:S(2)}, u32[]{:S(2)}) collective-permute-start(bf16[64,768]{1,0:T(8,128)(2,1)S(1)} %slice.209), channel_id=1, source_target_pairs={{0,16},{1,17},{2,18},{3,19},{4,20},{5,21},{6,22},{7,23},{8,24},{9,... | collective-permute-start | bytes 294920 | tf_op jit(solution)/shard_map/ppermute | solution.py:55
  263.0 16.0 %collective-permute-done.24 = bf16[784,768]{1,0:T(8,128)(2,1)} collective-permute-done((bf16[784,768]{1,0:T(8,128)(2,1)}, bf16[784,768]{1,0:T(8,128)(2,1)}, u32[]{:S(2)}, u32[]{:S(2)}) %collective-permute-start.24) | collective-permute-done | bytes 1204256 | tf_op jit(solution)/shard_map/ppermute | solution.py:55
  (161 shorter events, 101.5 us)
Async XLA Ops:
  8.2 34.5 %collective-permute-start.4 = (bf16[768,768]{1,0:T(8,128)(2,1)}, bf16[768,768]{1,0:T(8,128)(2,1)}, u32[]{:S(2)}, u32[]{:S(2)}) collective-permute-start(bf16[768,768]{1,0:T(8,128)(2,1)} %param.9), channel_id=1, source_target_pairs={{0,16},{1,17},{2,18},{3,19},{4,20},{5,21},{6,22},{7,23},{8,24},{9,... | collective-permute-start | bytes 3538952 | tf_op jit(solution)/shard_map/ppermute | solution.py:55
  8.3 34.4 %collective-permute-start.5 = (bf16[768,768]{1,0:T(8,128)(2,1)}, bf16[768,768]{1,0:T(8,128)(2,1)}, u32[]{:S(2)}, u32[]{:S(2)}) collective-permute-start(bf16[768,768]{1,0:T(8,128)(2,1)} %param.11), channel_id=1, source_target_pairs={{0,16},{1,17},{2,18},{3,19},{4,20},{5,21},{6,22},{7,23},{8,24},{9,... | collective-permute-start | bytes 3538952 | tf_op jit(solution)/shard_map/ppermute | solution.py:55
  10.0 14.0 %collective-permute-start.3 = (bf16[64,1536]{1,0:T(8,128)(2,1)}, bf16[64,1536]{1,0:T(8,128)(2,1)}, u32[]{:S(2)}, u32[]{:S(2)}) collective-permute-start(bf16[64,1536]{1,0:T(8,128)(2,1)} %pad_maximum_fusion.9), channel_id=1, source_target_pairs={{0,4},{1,5},{2,6},{3,7},{4,8},{5,9},{6,10},{7,11},{8,12},{9,13},{1... | collective-permute-start | bytes 589832 | tf_op jit(solution)/shard_map/ppermute | solution.py:55
  11.3 17.3 %collective-permute-start.2 = (bf16[64,1536]{1,0:T(8,128)(2,1)}, bf16[64,1536]{1,0:T(8,128)(2,1)}, u32[]{:S(2)}, u32[]{:S(2)}) collective-permute-start(bf16[64,1536]{1,0:T(8,128)(2,1)} %pad_maximum_fusion.9), channel_id=1, source_target_pairs={{0,8},{1,9},{2,10},{3,11},{4,12},{5,13},{6,14},{7,15},{8,0},{9,1},... | collective-permute-start | bytes 589832 | tf_op jit(solution)/shard_map/ppermute | solution.py:55
  16.4 18.9 %collective-permute-start.1 = (bf16[64,1536]{1,0:T(8,128)(2,1)}, bf16[64,1536]{1,0:T(8,128)(2,1)}, u32[]{:S(2)}, u32[]{:S(2)}) collective-permute-start(bf16[64,1536]{1,0:T(8,128)(2,1)} %pad_maximum_fusion.9), channel_id=1, source_target_pairs={{0,12},{1,13},{2,14},{3,15},{4,0},{5,1},{6,2},{7,3},{8,4},{9,5},{1... | collective-permute-start | bytes 589832 | tf_op jit(solution)/shard_map/ppermute | solution.py:55
  19.7 20.6 %all-to-all-start = ((bf16[4,64,1536]{2,1,0:T(8,128)(2,1)}), bf16[4,64,1536]{2,1,0:T(8,128)(2,1)}, u32[]{:S(2)}, u32[]{:S(2)}) async-start(bf16[4,64,1536]{2,1,0:T(8,128)(2,1)} %broadcast_in_dim.15), calls=%async_computation | async-start | bytes 1572864 | tf_op jit(solution)/shard_map/all_to_all | solution.py:97
  36.5 19.2 %collective-permute-start.8 = (bf16[256,1536]{1,0:T(8,128)(2,1)S(1)}, bf16[256,1536]{1,0:T(8,128)(2,1)}, u32[]{:S(2)}, u32[]{:S(2)}) collective-permute-start(bf16[256,1536]{1,0:T(8,128)(2,1)S(1)} %pad_maximum_fusion.6), channel_id=1, source_target_pairs={{0,3},{1,0},{2,1},{3,2},{4,7},{5,4},{6,5},{7,6},{8,11},{9,8},{10,9... | collective-permute-start | bytes 2359304 | tf_op jit(solution)/shard_map/ppermute | solution.py:55
  39.3 19.6 %collective-permute-start.9 = (bf16[256,1536]{1,0:T(8,128)(2,1)S(1)}, bf16[256,1536]{1,0:T(8,128)(2,1)}, u32[]{:S(2)}, u32[]{:S(2)}) collective-permute-start(bf16[256,1536]{1,0:T(8,128)(2,1)S(1)} %pad_maximum_fusion.6), channel_id=1, source_target_pairs={{0,1},{1,2},{2,3},{3,0},{4,5},{5,6},{6,7},{7,4},{8,9},{9,10},{10,1... | collective-permute-start | bytes 2359304 | tf_op jit(solution)/shard_map/ppermute | solution.py:55
  42.7 40.1 %collective-permute-start.6 = (bf16[4,64,1536]{2,1,0:T(8,128)(2,1)}, bf16[4,64,1536]{2,1,0:T(8,128)(2,1)}, u32[]{:S(2)}, u32[]{:S(2)}) collective-permute-start(bf16[4,64,1536]{2,1,0:T(8,128)(2,1)} %fusion.16), channel_id=1, source_target_pairs={{0,12},{1,13},{2,14},{3,15},{4,0},{5,1},{6,2},{7,3},{8,4},{9,5},{1... | collective-permute-start | bytes 2359304 | tf_op jit(solution)/shard_map/ppermute | solution.py:55
  46.1 36.8 %collective-permute-start.7 = (bf16[4,64,1536]{2,1,0:T(8,128)(2,1)}, bf16[4,64,1536]{2,1,0:T(8,128)(2,1)}, u32[]{:S(2)}, u32[]{:S(2)}) collective-permute-start(bf16[4,64,1536]{2,1,0:T(8,128)(2,1)} %fusion.16), channel_id=1, source_target_pairs={{0,4},{1,5},{2,6},{3,7},{4,8},{5,9},{6,10},{7,11},{8,12},{9,13},{1... | collective-permute-start | bytes 2359304 | tf_op jit(solution)/shard_map/ppermute | solution.py:55
  76.1 22.1 %all-to-all-start.1 = ((bf16[4,4,64,768]{3,2,1,0:T(8,128)(2,1)}), bf16[4,4,64,768]{3,2,1,0:T(8,128)(2,1)S(1)}, u32[]{:S(2)}, u32[]{:S(2)}) async-start(bf16[4,4,64,768]{3,2,1,0:T(8,128)(2,1)} %pad_maximum_fusion), calls=%async_computation.1 | async-start | bytes 3145728 | tf_op jit(solution)/shard_map/all_to_all | solution.py:76
  84.8 21.9 %collective-permute-start.13 = (bf16[2,64,1536]{2,1,0:T(8,128)(2,1)}, bf16[2,64,1536]{2,1,0:T(8,128)(2,1)}, u32[]{:S(2)}, u32[]{:S(2)}) collective-permute-start(bf16[2,64,1536]{2,1,0:T(8,128)(2,1)} %slice.146), channel_id=1, source_target_pairs={{0,4},{1,5},{2,6},{3,7},{4,8},{5,9},{6,10},{7,11},{8,12},{9,13},{1... | collective-permute-start | bytes 1179656 | tf_op jit(solution)/shard_map/ppermute | solution.py:55
  87.8 18.9 %collective-permute-start.12 = (bf16[2,64,1536]{2,1,0:T(8,128)(2,1)}, bf16[2,64,1536]{2,1,0:T(8,128)(2,1)}, u32[]{:S(2)}, u32[]{:S(2)}) collective-permute-start(bf16[2,64,1536]{2,1,0:T(8,128)(2,1)} %slice.145), channel_id=1, source_target_pairs={{0,12},{1,13},{2,14},{3,15},{4,0},{5,1},{6,2},{7,3},{8,4},{9,5},{1... | collective-permute-start | bytes 1179656 | tf_op jit(solution)/shard_map/ppermute | solution.py:55
  100.1 21.6 %all-to-all-start.2 = ((bf16[4,4,64,768]{3,2,1,0:T(8,128)(2,1)}), bf16[4,4,64,768]{3,2,1,0:T(8,128)(2,1)}, u32[]{:S(2)}, u32[]{:S(2)}) async-start(bf16[4,4,64,768]{3,2,1,0:T(8,128)(2,1)} %broadcast_in_dim.16), calls=%async_computation.2 | async-start | bytes 3145728 | tf_op jit(solution)/shard_map/all_to_all | solution.py:76
  130.1 24.3 %all-to-all-start.3 = ((bf16[4,4,64,768]{3,2,1,0:T(8,128)(2,1)}), bf16[4,4,64,768]{3,2,1,0:T(8,128)(2,1)S(1)}, u32[]{:S(2)}, u32[]{:S(2)}) async-start(bf16[4,4,64,768]{3,2,1,0:T(8,128)(2,1)} %pad_maximum_fusion.1), calls=%async_computation.3 | async-start | bytes 3145728 | tf_op jit(solution)/shard_map/all_to_all | solution.py:76
  156.5 23.3 %all-to-all-start.4 = ((bf16[4,4,64,768]{3,2,1,0:T(8,128)(2,1)}), bf16[4,4,64,768]{3,2,1,0:T(8,128)(2,1)S(1)}, u32[]{:S(2)}, u32[]{:S(2)}) async-start(bf16[4,4,64,768]{3,2,1,0:T(8,128)(2,1)} %broadcast_in_dim.17), calls=%async_computation.4 | async-start | bytes 3145728 | tf_op jit(solution)/shard_map/all_to_all | solution.py:76
  160.0 27.1 %collective-permute-start.15 = (bf16[768,768]{1,0:T(8,128)(2,1)}, bf16[768,768]{1,0:T(8,128)(2,1)}, u32[]{:S(2)}, u32[]{:S(2)}) collective-permute-start(bf16[768,768]{1,0:T(8,128)(2,1)} %add_convert_fusion.1), channel_id=1, source_target_pairs={{0,128},{1,129},{2,130},{3,131},{4,132},{5,133},{6,134},{7,135},{8... | collective-permute-start | bytes 3538952 | tf_op jit(solution)/shard_map/ppermute | solution.py:55
  193.1 37.3 %collective-permute-start.16 = (bf16[256,1536]{1,0:T(8,128)(2,1)S(1)}, bf16[256,1536]{1,0:T(8,128)(2,1)S(1)}, u32[]{:S(2)}, u32[]{:S(2)}) collective-permute-start(bf16[256,1536]{1,0:T(8,128)(2,1)S(1)} %convolution_convert_fusion.2), channel_id=1, source_target_pairs={{0,1},{1,2},{2,3},{3,0},{4,5},{5,6},{6,7},{7,4},{8,9},{9,10},{10,1... | collective-permute-start | bytes 2359304 | tf_op jit(solution)/shard_map/ppermute | solution.py:55
  194.1 36.4 %collective-permute-start.17 = (bf16[256,1536]{1,0:T(8,128)(2,1)S(1)}, bf16[256,1536]{1,0:T(8,128)(2,1)S(1)}, u32[]{:S(2)}, u32[]{:S(2)}) collective-permute-start(bf16[256,1536]{1,0:T(8,128)(2,1)S(1)} %convolution_convert_fusion.1), channel_id=1, source_target_pairs={{0,3},{1,0},{2,1},{3,2},{4,7},{5,4},{6,5},{7,6},{8,11},{9,8},{10,9... | collective-permute-start | bytes 2359304 | tf_op jit(solution)/shard_map/ppermute | solution.py:55
  197.6 32.8 %collective-permute-start.18 = (bf16[256,1536]{1,0:T(8,128)(2,1)S(1)}, bf16[256,1536]{1,0:T(8,128)(2,1)S(1)}, u32[]{:S(2)}, u32[]{:S(2)}) collective-permute-start(bf16[256,1536]{1,0:T(8,128)(2,1)S(1)} %convolution_convert_fusion), channel_id=1, source_target_pairs={{0,2},{1,3},{2,0},{3,1},{4,6},{5,7},{6,4},{7,5},{8,10},{9,11},{10,... | collective-permute-start | bytes 2359304 | tf_op jit(solution)/shard_map/ppermute | solution.py:55
  232.1 17.2 %collective-permute-start.22 = (bf16[64,1536]{1,0:T(8,128)(2,1)}, bf16[64,1536]{1,0:T(8,128)(2,1)S(1)}, u32[]{:S(2)}, u32[]{:S(2)}) collective-permute-start(bf16[64,1536]{1,0:T(8,128)(2,1)} %get-tuple-element.53), channel_id=1, source_target_pairs={{0,12},{1,13},{2,14},{3,15},{4,0},{5,1},{6,2},{7,3},{8,4},{9,5},{1... | collective-permute-start | bytes 589832 | tf_op jit(solution)/shard_map/ppermute | solution.py:55
  235.4 13.9 %collective-permute-start.21 = (bf16[64,1536]{1,0:T(8,128)(2,1)S(1)}, bf16[64,1536]{1,0:T(8,128)(2,1)S(1)}, u32[]{:S(2)}, u32[]{:S(2)}) collective-permute-start(bf16[64,1536]{1,0:T(8,128)(2,1)S(1)} %get-tuple-element.54), channel_id=1, source_target_pairs={{0,8},{1,9},{2,10},{3,11},{4,12},{5,13},{6,14},{7,15},{8,0},{9,1},... | collective-permute-start | bytes 589832 | tf_op jit(solution)/shard_map/ppermute | solution.py:55
  236.6 16.1 %collective-permute-start.20 = (bf16[64,1536]{1,0:T(8,128)(2,1)S(1)}, bf16[64,1536]{1,0:T(8,128)(2,1)}, u32[]{:S(2)}, u32[]{:S(2)}) collective-permute-start(bf16[64,1536]{1,0:T(8,128)(2,1)S(1)} %get-tuple-element.52), channel_id=1, source_target_pairs={{0,4},{1,5},{2,6},{3,7},{4,8},{5,9},{6,10},{7,11},{8,12},{9,13},{1... | collective-permute-start | bytes 589832 | tf_op jit(solution)/shard_map/ppermute | solution.py:55
  237.5 41.5 %collective-permute-start.24 = (bf16[784,768]{1,0:T(8,128)(2,1)}, bf16[784,768]{1,0:T(8,128)(2,1)}, u32[]{:S(2)}, u32[]{:S(2)}) collective-permute-start(bf16[784,768]{1,0:T(8,128)(2,1)} %pad_maximum_fusion.5), channel_id=1, source_target_pairs={{0,128},{1,129},{2,130},{3,131},{4,132},{5,133},{6,134},{7,135},{8... | collective-permute-start | bytes 3612680 | tf_op jit(solution)/shard_map/ppermute | solution.py:55
  (35 other events, 252.2 us)
